TPU v7x, 32 devices: a whole 2x2x4 slice. The times are simulated.
32 devices in a mesh: seq: 4 (over y, x), tensor: 8 (over z, core).
Axes of the slice: x: 2, y: 2, z: 4, core: 2. Of those that a mesh axis runs over, the one named last changes fastest.
Arguments:
- hidden_in: bfloat16 [4096, 2304], P(('seq', 'tensor')), may hold values from -6 to 6
- norm_attn: float32 [2304], replicated, may hold values from 0.1 to 1.9
- norm_ffn: float32 [2304], replicated, may hold values from 0.1 to 1.9
- w_qkv: bfloat16 [3, 2304, 512], P(None, None, 'tensor'), may hold values from -1 to 1
- w_out: bfloat16 [512, 2304], P('tensor'), may hold values from -0.25 to 0.25
- w_router: float32 [2304, 8], replicated, may hold values from -4 to 4
- w_gate_up: bfloat16 [2, 23040, 2304], P(None, 'tensor'), may hold values from -0.125 to 0.125
- w_down: bfloat16 [23040, 2304], P('tensor'), may hold values from -0.109375 to 0.109375
- segment_ids: int32 [4096], P('seq'), may hold values from 0 to 7, never falling along the last dimension, each value on 1 to 3072 neighbouring positions
- expert_ids: int32 [4096, 2], P(('seq', 'tensor')), may hold values from 0 to 7, all different within a row; in each aligned block of 128 rows (0 to 127, 128 to 255, ...) at most 64 rows name the same one
Outputs:
- hidden_out: bfloat16 [4096, 2304], P(('seq', 'tensor'))
- kv_cache: bfloat16 [8, 4096, 128], P('tensor', 'seq')
Inputs may be any that keep to these rules, and one draw needn't show every extreme that they name: `segment_ids`: nondecreasing along the stream; each prompt has 1 to 3072 tokens and one has exactly 3072. `expert_ids`: the two experts of a token differ. Within each aligned block of 128 tokens (the tokens of one device), no expert is named by more than 64 tokens, a bound that some block reaches.
All inputs are finite; a program needn't handle non-finite values.
Results may differ from a plain program's by a relative error of at most 0.019.
Values may be sent and summed in bfloat16 or wider, within the bound.
A program may use at most 128 MiB of HBM per device.

v0:
```python
import math
import jax
import jax.numpy as jnp
from jax import lax
from jax.sharding import PartitionSpec as P

HD = 64
epsilon = 1e-06
low_score = -1e30


def rms_norm(hidden_rows, gain):
    as_float = hidden_rows.astype(jnp.float32)
    scale = lax.rsqrt(jnp.mean(as_float * as_float, axis=-1, keepdims=True) + epsilon)
    return (as_float * scale * gain).astype(jnp.bfloat16)


def rotate(head_rows, positions):
    half_size = head_rows.shape[-1] // 2
    frequency = jnp.exp(jnp.arange(half_size, dtype=jnp.float32) * (-math.log(10000.0) / half_size))
    angles = positions.astype(jnp.float32)[:, None] * frequency[None, :]
    cosine = jnp.cos(angles)[:, None, :]
    sine_part = jnp.sin(angles)[:, None, :]
    front_half = head_rows[..., :half_size]
    back_half = head_rows[..., half_size:]
    return jnp.concatenate(
        [front_half * cosine - back_half * sine_part, back_half * cosine + front_half * sine_part],
        axis=-1,
    )


def fold_keys(
    softmax_state, query_rows, query_segments, query_positions, kv_rows, key_segments, key_start
):
    running_max, denominator, weighted_sum = softmax_state
    row_count = kv_rows.shape[0]
    block_size = math.gcd(row_count, 2048)
    head_size = query_rows.shape[-1]
    for block_start in range(0, row_count, block_size):
        kv_block = kv_rows[block_start : block_start + block_size]
        key_block = kv_block[..., :head_size]
        value_block = kv_block[..., head_size:]
        segment_block = key_segments[block_start : block_start + block_size]
        position_block = key_start + block_start + jnp.arange(block_size, dtype=jnp.int32)
        scores = (
            jnp.einsum("qhd,khd->hqk", query_rows, key_block, preferred_element_type=jnp.float32)
            * 0.125
        )
        allowed = (query_segments[:, None] == segment_block[None, :]) & (
            position_block[None, :] <= query_positions[:, None]
        )
        masked = jnp.where(allowed[None], scores, low_score)
        new_max = jnp.maximum(running_max, jnp.max(masked, axis=-1))
        weights = jnp.where(allowed[None], jnp.exp(masked - new_max[..., None]), 0.0)
        factor = jnp.exp(running_max - new_max)
        denominator = denominator * factor + jnp.sum(weights, axis=-1)
        weighted_sum = weighted_sum * factor[..., None] + jnp.einsum(
            "hqk,khd->hqd",
            weights.astype(jnp.bfloat16),
            value_block,
            preferred_element_type=jnp.float32,
        )
        running_max = new_max
    return (running_max, denominator, weighted_sum)


def slot_table(token_ids, target, slot_count):
    is_routed = jnp.any(token_ids == target, axis=1).astype(jnp.int32)
    places = jnp.arange(is_routed.shape[0], dtype=jnp.int32)
    slot_rank = (
        jnp.sum(jnp.where(places[None, :] <= places[:, None], is_routed[None, :], 0), axis=1) - 1
    )
    chosen_slot = (is_routed[None, :] == 1) & (
        slot_rank[None, :] == jnp.arange(slot_count, dtype=jnp.int32)[:, None]
    )
    return chosen_slot.astype(jnp.bfloat16)


def expert_apply(slot_rows, slot_ids, own_expert, w_router, w_gate_up, w_down):
    logits = jnp.dot(slot_rows.astype(jnp.float32), w_router, precision=lax.Precision.HIGHEST)
    expert_count = w_router.shape[1]
    one_hot = (
        slot_ids[:, :, None] == jnp.arange(expert_count, dtype=jnp.int32)[None, None, :]
    ).astype(jnp.float32)
    chosen = jnp.sum(one_hot * logits[:, None, :], axis=-1)
    gate_probs = jax.nn.softmax(chosen, axis=-1)
    weight = jnp.sum(jnp.where(slot_ids == own_expert, gate_probs, 0.0), axis=-1)
    contract = (((1,), (1,)), ((), ()))
    gate_act = lax.dot_general(
        slot_rows, w_gate_up[0], contract, preferred_element_type=jnp.float32
    )
    up_act = lax.dot_general(slot_rows, w_gate_up[1], contract, preferred_element_type=jnp.float32)
    hidden_act = (jax.nn.silu(gate_act) * up_act).astype(jnp.bfloat16)
    output = jnp.dot(hidden_act, w_down, preferred_element_type=jnp.float32)
    return (output * weight[:, None]).astype(jnp.bfloat16)


def shards(
    hidden_in,
    norm_attn,
    norm_ffn,
    w_qkv,
    w_out,
    w_router,
    w_gate_up,
    w_down,
    segment_ids,
    expert_ids,
):
    local_rows = hidden_in.shape[0]
    model_width = hidden_in.shape[1]
    tensor_count = lax.axis_size("tensor")
    tensor_place = lax.axis_index("tensor")
    seq_place = lax.axis_index("seq")
    group_rows = local_rows * tensor_count
    head_count = w_qkv.shape[2] // HD
    normed = rms_norm(hidden_in, norm_attn)
    projected = jnp.einsum(
        "td,cdh->tch",
        lax.all_gather(normed, "tensor", axis=0, tiled=True),
        w_qkv,
        preferred_element_type=jnp.float32,
    )
    positions = seq_place * group_rows + jnp.arange(group_rows, dtype=jnp.int32)
    query_rows = rotate(projected[:, 0].reshape(group_rows, head_count, HD), positions).astype(
        jnp.bfloat16
    )
    key_rows = rotate(projected[:, 1].reshape(group_rows, head_count, HD), positions).astype(
        jnp.bfloat16
    )
    value_rows = projected[:, 2].reshape(group_rows, head_count, HD).astype(jnp.bfloat16)
    kv_rows = jnp.concatenate([key_rows, value_rows], axis=-1)
    kv_cache = kv_rows.transpose(1, 0, 2)
    start_state = (
        jnp.full((head_count, group_rows), low_score, jnp.float32),
        jnp.zeros((head_count, group_rows), jnp.float32),
        jnp.zeros((head_count, group_rows, HD), jnp.float32),
    )
    softmax_state = fold_keys(
        start_state,
        query_rows,
        segment_ids,
        positions,
        lax.all_gather(kv_rows, "seq", axis=0, tiled=True),
        lax.all_gather(segment_ids, "seq", axis=0, tiled=True),
        jnp.int32(0),
    )
    running_max, denominator, weighted_sum = softmax_state
    attended = (
        (weighted_sum / denominator[..., None])
        .transpose(1, 0, 2)
        .reshape(group_rows, head_count * HD)
        .astype(jnp.bfloat16)
    )
    attention_sum = lax.psum_scatter(
        jnp.dot(attended, w_out, preferred_element_type=jnp.float32).astype(jnp.bfloat16),
        "tensor",
        scatter_dimension=0,
        tiled=True,
    ).astype(jnp.float32)
    residual = hidden_in.astype(jnp.float32) + attention_sum
    normed_ffn = rms_norm(residual, norm_ffn)
    expert_count = w_router.shape[1]
    slice_count = tensor_count // expert_count
    own_expert = tensor_place // slice_count
    slot_count = local_rows // 2
    full_rows, full_ids = (
        lax.all_gather(normed_ffn, "tensor", axis=0, tiled=True),
        lax.all_gather(expert_ids, "tensor", axis=0, tiled=True),
    )
    block_ids = full_ids.reshape(tensor_count, local_rows, 2)
    slot_tables = jax.vmap(lambda source_ids: slot_table(source_ids, own_expert, slot_count))(
        block_ids
    )
    slot_rows = jnp.einsum(
        "sjr,srd->sjd",
        slot_tables,
        full_rows.reshape(tensor_count, local_rows, model_width),
        preferred_element_type=jnp.float32,
    ).astype(jnp.bfloat16)
    slot_ids = jnp.einsum(
        "sjr,srk->sjk", slot_tables.astype(jnp.float32), block_ids.astype(jnp.float32)
    ).astype(jnp.int32)
    term_rows = expert_apply(
        slot_rows.reshape(-1, model_width),
        slot_ids.reshape(-1, 2),
        own_expert,
        w_router,
        w_gate_up,
        w_down,
    )
    placed = jnp.einsum(
        "sjr,sjd->srd",
        slot_tables,
        term_rows.reshape(tensor_count, slot_count, model_width),
        preferred_element_type=jnp.float32,
    ).reshape(group_rows, model_width)
    expert_sum = lax.psum_scatter(
        placed.astype(jnp.bfloat16), "tensor", scatter_dimension=0, tiled=True
    ).astype(jnp.float32)
    hidden_out = (residual + expert_sum).astype(jnp.bfloat16)
    return (hidden_out, kv_cache)


def solution(mesh):
    placed = (
        P(("seq", "tensor"), None),
        P(),
        P(),
        P(None, None, "tensor"),
        P("tensor", None),
        P(),
        P(None, "tensor", None),
        P("tensor", None),
        P("seq"),
        P(("seq", "tensor"), None),
    )
    return jax.shard_map(
        shards,
        mesh=mesh,
        in_specs=placed,
        out_specs=(P(("seq", "tensor"), None), P("tensor", "seq", None)),
        check_vma=False,
    )
```

profile of v0, /device:TPU:0, one launch (start us, length us, event | category | flops | bytes accessed | tf_op | source)
XLA Modules:
  0.0 339.1 jit_solution(13860457289444476095)
XLA Ops:
  7.2 1.3 fusion.20
  8.6 2.1 fusion.22
  10.8 54.5 %all-gather.4.cloned.1.call-done = bf16[1024,2304]{1,0:T(8,128)(2,1)} async-done(((bf16[128,2304]{1,0:T(8,128)(2,1)}), bf16[1024,2304]{1,0:T(8,128)(2,1)}) %all-gather.4.cloned.1.call-update) | async-done | bytes 4718608 | tf_op jit(solution)/shard_map/all_gather | solution.py:120
  65.3 4.0 %fusion.95 = f32[1024,192]{0,1:S(1)} fusion(bf16[1024,2304]{1,0:T(8,128)(2,1)} %all-gather.4.cloned.1.call-done, bf16[2304,192]{0,1:T(8,128)(2,1)S(1)} %bitcast.62), kind=kOutput, calls=%fused_computation.120 | convolution fusion | flops 905969664 | bytes 6389760
  69.3 0.6 fusion.70
  69.9 0.8 fusion.93
  70.7 8.1 %all_gather.15 = s32[4096]{0:T(1024)S(1)} all-gather(s32[1024]{0:T(1024)S(1)} %copy-done.8), channel_id=1, replica_groups=mesh['seq'=4,'tensor'=8] {'seq'}, dimensions={0}, use_global_device_ids=true | all-gather | bytes 20480 | tf_op jit(solution)/shard_map/all_gather | solution.py:145
  78.9 17.4 %all-gather.6.cloned.1.call-done = bf16[4096,1,128]{0,2,1:T(8,128)(2,1)} async-done(((bf16[1024,1,128]{0,2,1:T(8,128)(2,1)}), bf16[4096,1,128]{0,2,1:T(8,128)(2,1)}) %all-gather.6.cloned.1.call-update) | async-done | bytes 1048592 | tf_op jit(solution)/shard_map/all_gather | solution.py:144
  96.3 2.3 fusion.41
  98.6 4.1 %fusion.8 = (f32[1024]{0:T(1024)S(1)}, f32[1024]{0:T(1024)S(1)}, f32[1024,2048]{1,0:T(8,128)S(1)}) fusion(s32[2048]{0:T(1024)S(1)} %iota_add_fusion, s32[2048]{0:T(1024)S(1)} %get-tuple-element.23, s32[1024]{0:T(1024)S(1)} %iota_add_fusion.1, s32[1024]{0:T(1024)S(1)} %copy-done.8, f32[1024,2048]{1,0:T(8,128)S(1)} %fusion.41, ...), kind=kOutput, calls=%fused_computation.14 | convolution fusion | flops 293861376 | bytes 17211392 | tf_op jit(solution)/shard_map/qhd,khd->hqk/dot_general | solution.py:46
  102.7 6.2 %fusion.12 = (f32[1024]{0:T(1024)S(1)}, f32[1024]{0:T(1024)S(1)}) fusion(f32[1024,2048]{1,0:T(8,128)S(1)} %fusion.41, f32[1024]{0:T(1024)S(1)} %get-tuple-element.26, s32[2048]{0:T(1024)S(1)} %get-tuple-element.22, s32[1024]{0:T(1024)S(1)} %iota_add_fusion.1, s32[1024]{0:T(1024)S(1)} %copy-done.8, f32[1024]{0:T(1024)S(1)} %get-tuple-element.25, ...), kind=kLoop, calls=%fused_computation.21 | loop fusion | flops 33552384 | bytes 16826368 | tf_op jit(solution)/shard_map/reduce_sum | solution.py:56
  108.9 2.8 fusion.29
  111.7 8.0 %convolution_convert_fusion.1 = bf16[1024,2304]{1,0:T(8,128)(2,1)} fusion(bf16[64,2304]{1,0:T(8,128)(2,1)S(1)} %copy-done.11, f32[1024,64]{0,1:T(8,128)S(1)} %fusion.29, f32[1024,2048]{1,0:T(8,128)} %copy-done.4, f32[1024]{0:T(1024)S(1)} %get-tuple-element.25, s32[2048]{0:T(1024)S(1)} %iota_add_fusion, s32[2048]{0:T(1024)S(1)} %get-tuple-element.23, ...), kind=kOutput, calls=%fused_computation.17 | convolution fusion | flops 589758464 | bytes 13959168 | tf_op jit(solution)/shard_map/dot_general | solution.py:156
  119.8 0.2 all-gather.8.cloned.1.call-start
  120.0 54.9 %reduce-scatter.3.cloned.1.call-done = bf16[128,2304]{1,0:T(8,128)(2,1)} async-done(((bf16[1024,2304]{1,0:T(8,128)(2,1)}), bf16[128,2304]{1,0:T(8,128)(2,1)}) %reduce-scatter.3.cloned.1.call-update) | async-done | bytes 589840 | tf_op jit(solution)/shard_map/reduce_scatter | solution.py:155
  174.9 1.3 multiply_reduce_fusion
  176.2 2.1 multiply_convert_fusion.1
  178.4 9.2 %all_gather.18 = s32[1024,2]{0,1:T(2,128)S(1)} all-gather(s32[128,2]{0,1:T(2,128)S(1)} %copy-done.10), channel_id=1, replica_groups=mesh['seq'=4,'tensor'=8] {'tensor'}, dimensions={0}, use_global_device_ids=true | all-gather | bytes 9216 | tf_op jit(solution)/shard_map/all_gather | solution.py:169
  187.6 0.2 select_reduce_fusion
  187.9 0.2 fusion.77
  188.1 0.1 eq.91
  188.1 40.4 %all-gather.8.cloned.1.call-done = bf16[1024,2304]{1,0:T(8,128)(2,1)} async-done(((bf16[128,2304]{1,0:T(8,128)(2,1)}), bf16[1024,2304]{1,0:T(8,128)(2,1)}) %all-gather.8.cloned.1.call-update) | async-done | bytes 4718608 | tf_op jit(solution)/shard_map/all_gather | solution.py:168
  228.6 3.1 convolution_convert_fusion.2
  231.7 1.5 copy-done.3
  233.2 1.9 fusion.96
  235.1 0.1 reduce_sum.80
  235.3 12.5 %fusion.2 = f32[512,2880]{0,1:T(8,128)} fusion(bf16[512,2304]{1,0:T(8,128)(2,1)} %bitcast.65, bf16[2,2880,2304]{2,1,0:T(8,128)(2,1)} %param.16), kind=kOutput, calls=%fused_computation.2 | convolution fusion | flops 6794772480 | bytes 21528576 | tf_op jit(solution)/shard_map/dot_general | solution.py:89
  248.0 23.2 %fusion.11 = bf16[512,2304]{1,0:T(8,128)(2,1)} fusion(bf16[2880,2304]{1,0:T(8,128)(2,1)} %param.17, f32[512]{0:T(512)S(1)} %mul.193, f32[512,2880]{0,1:T(8,128)} %fusion.2, bf16[512,2304]{1,0:T(8,128)(2,1)} %bitcast.66, bf16[2,2880,2304]{2,1,0:T(8,128)(2,1)} %param.16), kind=kOutput, calls=%fused_computation.20 | convolution fusion | flops 13600751616 | bytes 37160960 | tf_op jit(solution)/shard_map/dot_general | solution.py:94
  271.2 5.3 %convolution_convert_fusion = bf16[8,128,2304]{2,1,0:T(8,128)(2,1)} fusion(bf16[8,64,2304]{2,1,0:T(8,128)(2,1)} %bitcast.68, s32[8,128]{1,0:T(8,128)S(1)} %broadcast_add_fusion, pred[8,128]{1,0:T(8,128)(4,1)S(1)} %broadcast_compare_fusion), kind=kOutput, calls=%fused_computation.16 | convolution fusion | flops 304480256 | bytes 7083008 | tf_op jit(solution)/shard_map/sjr,sjd->srd/dot_general | solution.py:192
  276.6 0.8 copy.26
  277.4 53.1 %reduce-scatter.5.cloned.1.call-done = bf16[128,2304]{1,0:T(8,128)(2,1)} async-done(((bf16[1024,2304]{1,0:T(8,128)(2,1)}), bf16[128,2304]{1,0:T(8,128)(2,1)}) %reduce-scatter.5.cloned.1.call-update) | async-done | bytes 589840 | tf_op jit(solution)/shard_map/reduce_scatter | solution.py:198
  330.5 2.1 add_convert_fusion
  (55 shorter events, 0.8 us)
Async XLA Ops:
  7.2 58.1 %copy-start = (bf16[3,2304,64]{1,2,0:T(8,128)(2,1)S(1)}, bf16[3,2304,64]{1,2,0:T(8,128)(2,1)}, u32[]{:S(2)}) copy-start(bf16[3,2304,64]{1,2,0:T(8,128)(2,1)} %param.13) | copy-start | bytes 2654212
  7.2 63.5 %copy-start.8 = (s32[1024]{0:T(1024)S(1)}, s32[1024]{0:T(1024)}, u32[]{:S(2)}) copy-start(s32[1024]{0:T(1024)} %param.18) | copy-start | bytes 12292
  7.2 58.1 %all-gather.4.cloned.1.call-start = ((), (), s32[]{:S(2)}) async-start(), calls=%async_computation.2 | async-start | bytes 5308416 | tf_op jit(solution)/shard_map/all_gather | solution.py:120
  10.7 85.6 %all-gather.6.cloned.1.call-start = ((), (), s32[]{:S(2)}) async-start(), calls=%async_computation.3 | async-start | bytes 1310720 | tf_op jit(solution)/shard_map/all_gather | solution.py:144
  70.7 104.2 %reduce-scatter.3.cloned.1.call-start = ((), (), s32[]{:S(2)}) async-start(), calls=%async_computation.4 | async-start | bytes 5308416 | tf_op jit(solution)/shard_map/reduce_scatter | solution.py:155
  96.3 2.3 copy-start.7
  102.7 6.2 %copy-start.4 = (f32[1024,2048]{1,0:T(8,128)}, f32[1024,2048]{1,0:T(8,128)S(1)}, u32[]{:S(2)}) copy-start(f32[1024,2048]{1,0:T(8,128)S(1)} %get-tuple-element.27) | copy-start | bytes 25165828
  108.9 2.8 copy-start.11
  111.7 63.2 %copy-start.2 = (bf16[128,2304]{1,0:T(8,128)(2,1)S(1)}, bf16[128,2304]{1,0:T(8,128)(2,1)}, u32[]{:S(2)}) copy-start(bf16[128,2304]{1,0:T(8,128)(2,1)} %param.10) | copy-start | bytes 1769476
  119.7 56.5 %copy-start.9 = (f32[2304]{0:T(1024)S(1)}, f32[2304]{0:T(1024)}, u32[]{:S(2)}) copy-start(f32[2304]{0:T(1024)} %param.12) | copy-start | bytes 27652
  119.7 58.7 %copy-start.10 = (s32[128,2]{0,1:T(2,128)S(1)}, s32[128,2]{0,1:T(2,128)}, u32[]{:S(2)}) copy-start(s32[128,2]{0,1:T(2,128)} %param.19) | copy-start | bytes 3076
  119.8 113.4 %copy-start.6 = (f32[2304,8]{0,1:T(8,128)S(1)}, f32[2304,8]{0,1:T(8,128)}, u32[]{:S(2)}) copy-start(f32[2304,8]{0,1:T(8,128)} %param.15) | copy-start | bytes 221188
  119.8 108.8 %all-gather.8.cloned.1.call-start = ((), (), s32[]{:S(2)}) async-start(), calls=%async_computation.5 | async-start | bytes 5308416 | tf_op jit(solution)/shard_map/all_gather | solution.py:168
  178.4 152.1 %reduce-scatter.5.cloned.1.call-start = ((), (), s32[]{:S(2)}) async-start(), calls=%async_computation.6 | async-start | bytes 5308416 | tf_op jit(solution)/shard_map/reduce_scatter | solution.py:198
  231.7 1.5 copy-start.3
  271.2 61.4 %copy-start.1 = (bf16[3,2304,64]{1,2,0:T(8,128)(2,1)S(1)}, bf16[3,2304,64]{1,2,0:T(8,128)(2,1)}, u32[]{:S(2)}) copy-start(bf16[3,2304,64]{1,2,0:T(8,128)(2,1)} %param.13) | copy-start | bytes 2654212
  271.2 59.3 %copy-start.5 = (bf16[128,2304]{1,0:T(8,128)(2,1)S(1)}, bf16[128,2304]{1,0:T(8,128)(2,1)}, u32[]{:S(2)}) copy-start(bf16[128,2304]{1,0:T(8,128)(2,1)} %reduce-scatter.3.cloned.1.call-done) | copy-start | bytes 1769476
Sparse Core Ops, SparseCore 0:
  10.8 54.3 all-gather.3
  70.8 25.4 all-gather.5
  119.9 54.9 reduce-scatter.2
  178.5 50.0 all-gather.7
  276.7 53.7 reduce-scatter.4
where the time goes:
time: 340 us; the launch traced here: 339 us
  waiting for transfers between devices  220 us (65%)
  matrix products  67.4 us (20%)
  blocking collectives  17.3 us (5%)
  other arithmetic  16.9 us (5%)
  between operations  14 us (4%)
    reduce_scatter x1, waiting for transfers between devices, shards(): lax.psum_scatter(jnp.dot(attended, w_out, preferred_element_type=jnp.floa...  54.9 us
    all_gather x1, waiting for transfers between devices, shards(): lax.all_gather(normed, 'tensor', axis=0, tiled=True)  54.5 us
    reduce_scatter x1, waiting for transfers between devices, shards(): lax.psum_scatter(placed.astype(jnp.bfloat16), 'tensor', scatter_dimension...  53.1 us
    all_gather x1, waiting for transfers between devices, shards(): lax.all_gather(normed_ffn, 'tensor', axis=0, tiled=True)  40.4 us
    dot_general x1, matrix products, expert_apply(): output = jnp.dot(hidden_act, w_down, preferred_element_type=jnp.float32)  23.2 us
    all_gather x1, waiting for transfers between devices, shards(): lax.all_gather(kv_rows, 'seq', axis=0, tiled=True)  17.4 us
    dot_general x1, matrix products, expert_apply(): lax.dot_general(slot_rows, w_gate_up[0], contract, preferred_element_type...  12.5 us
    all_gather x1, blocking collectives, shards(): lax.all_gather(expert_ids, 'tensor', axis=0, tiled=True)  9.15 us
  transfers between devices with their start and end apart: 5, of which 5 were waited for; matrix products, arithmetic and copies ran while one was open for 0% of the time, Pallas kernels for 0%

commit v1 on v0

--- a/solution.py
+++ b/solution.py
@@ -7,6 +7,19 @@
 HD = 64
 epsilon = 1e-06
 low_score = -1e30
+
+
+def gather_around(value, axis, dim):
+    ways = lax.axis_size(axis)
+    up = [(d, (d + 1) % ways) for d in range(ways)]
+    down = [(d, (d - 1) % ways) for d in range(ways)]
+    earlier, later = ([value], [value])
+    for _ in range(ways // 2):
+        earlier.append(lax.ppermute(earlier[-1], axis, up))
+    for _ in range((ways - 1) // 2):
+        later.append(lax.ppermute(later[-1], axis, down))
+    line = jnp.concatenate([*earlier[::-1], *later[1:]], axis=dim)
+    return jnp.roll(line, (lax.axis_index(axis) - ways // 2) * value.shape[dim], axis=dim)
 
 
 def rms_norm(hidden_rows, gain):
@@ -165,7 +178,7 @@
     own_expert = tensor_place // slice_count
     slot_count = local_rows // 2
     full_rows, full_ids = (
-        lax.all_gather(normed_ffn, "tensor", axis=0, tiled=True),
+        gather_around(normed_ffn, "tensor", 0),
         lax.all_gather(expert_ids, "tensor", axis=0, tiled=True),
     )
     block_ids = full_ids.reshape(tensor_count, local_rows, 2)

time: 340 us -> 358 us (1.053)
  starting transfers between devices: 0.39 us -> 8.92 us
  local copies, waits for them, and re-layouts: 2.76 us -> 10.1 us
  blocking collectives: 17.3 us -> 20.9 us
    all_gather x1 -> x0, waiting for transfers between devices: 40.4 us -> none  [shards(): lax.all_gather(normed_ffn, 'tensor', axis=0, tiled=True)]
    ppermute x0 -> x7, waiting for transfers between devices: none -> 39.5 us  [the longest x4 22.4 us: gather_around(): earlier.append(lax.ppermute(earlier[-1], axis, up))]
    ppermute x0 -> x7, starting transfers between devices: none -> 8.76 us  [the longest x3 8.69 us: gather_around(): later.append(lax.ppermute(later[-1], axis, down))]
    unnamed x25 -> x40, local copies, waits for them, and re-layouts: 2.36 us -> 9.35 us
    all_gather x1, blocking collectives: 9.15 us -> 12.8 us  [shards(): lax.all_gather(expert_ids, 'tensor', axis=0, tiled=True)]
  transfers between devices with their start and end apart: 5 -> 11, of which waited for: 5 -> 8; matrix products, arithmetic and copies ran while one was open for 0% -> 1% of each run, Pallas kernels for 0% -> 0%
where the time goes in v1:
time: 358 us; the launch traced here: 357 us
  waiting for transfers between devices  222 us (62%)
  matrix products  65.1 us (18%)
  blocking collectives  20.9 us (6%)
  other arithmetic  16.1 us (4%)
  between operations  14.1 us (4%)
  local copies, waits for them, and re-layouts  10.1 us (3%)
  starting transfers between devices  8.92 us (2%)
    reduce_scatter x1, waiting for transfers between devices, shards(): lax.psum_scatter(placed.astype(jnp.bfloat16), 'tensor', scatter_dimension...  55.5 us
    reduce_scatter x1, waiting for transfers between devices, shards(): lax.psum_scatter(jnp.dot(attended, w_out, preferred_element_type=jnp.floa...  55.1 us
    all_gather x1, waiting for transfers between devices, shards(): lax.all_gather(normed, 'tensor', axis=0, tiled=True)  54.5 us
    dot_general x1, matrix products, expert_apply(): output = jnp.dot(hidden_act, w_down, preferred_element_type=jnp.float32)  23.3 us
    ppermute x4, waiting for transfers between devices, gather_around(): earlier.append(lax.ppermute(earlier[-1], axis, up))  22.4 us
    all_gather x1, waiting for transfers between devices, shards(): lax.all_gather(kv_rows, 'seq', axis=0, tiled=True)  17.4 us
    ppermute x3, waiting for transfers between devices, gather_around(): later.append(lax.ppermute(later[-1], axis, down))  17.1 us
    all_gather x1, blocking collectives, shards(): lax.all_gather(expert_ids, 'tensor', axis=0, tiled=True)  12.8 us
  transfers between devices with their start and end apart: 11, of which 8 were waited for; matrix products, arithmetic and copies ran while one was open for 1% of the time, Pallas kernels for 0%

profile of v1, /device:TPU:0, one launch (start us, length us, event | category | flops | bytes accessed | tf_op | source)
XLA Modules:
  0.0 357.3 jit_solution(2976614681670291241)
XLA Ops:
  7.2 1.3 fusion.20
  8.6 2.1 fusion.22
  10.8 54.5 %all-gather.3.cloned.1.call-done = bf16[1024,2304]{1,0:T(8,128)(2,1)} async-done(((bf16[128,2304]{1,0:T(8,128)(2,1)}), bf16[1024,2304]{1,0:T(8,128)(2,1)}) %all-gather.3.cloned.1.call-update) | async-done | bytes 4718608 | tf_op jit(solution)/shard_map/all_gather | solution.py:133
  65.3 4.0 %fusion.95 = f32[1024,192]{0,1:S(1)} fusion(bf16[1024,2304]{1,0:T(8,128)(2,1)} %all-gather.3.cloned.1.call-done, bf16[2304,192]{0,1:T(8,128)(2,1)S(1)} %bitcast.62), kind=kOutput, calls=%fused_computation.137 | convolution fusion | flops 905969664 | bytes 6389760
  70.7 8.1 %all_gather.12 = s32[4096]{0:T(1024)S(1)} all-gather(s32[1024]{0:T(1024)S(1)} %copy-done.8), channel_id=1, replica_groups=mesh['seq'=4,'tensor'=8] {'seq'}, dimensions={0}, use_global_device_ids=true | all-gather | bytes 20480 | tf_op jit(solution)/shard_map/all_gather | solution.py:158
  78.9 17.4 %all-gather.5.cloned.1.call-done = bf16[4096,1,128]{0,2,1:T(8,128)(2,1)} async-done(((bf16[1024,1,128]{0,2,1:T(8,128)(2,1)}), bf16[4096,1,128]{0,2,1:T(8,128)(2,1)}) %all-gather.5.cloned.1.call-update) | async-done | bytes 1048592 | tf_op jit(solution)/shard_map/all_gather | solution.py:157
  96.3 2.3 fusion.41
  98.6 4.1 %fusion.8 = (f32[1024]{0:T(1024)S(1)}, f32[1024]{0:T(1024)S(1)}, f32[1024,2048]{1,0:T(8,128)S(1)}) fusion(s32[2048]{0:T(1024)S(1)} %iota_add_fusion, s32[2048]{0:T(1024)S(1)} %get-tuple-element.23, s32[1024]{0:T(1024)S(1)} %iota_add_fusion.1, s32[1024]{0:T(1024)S(1)} %copy-done.8, f32[1024,2048]{1,0:T(8,128)S(1)} %fusion.41, ...), kind=kOutput, calls=%fused_computation.14 | convolution fusion | flops 293861376 | bytes 17211392 | tf_op jit(solution)/shard_map/qhd,khd->hqk/dot_general | solution.py:59
  102.7 6.2 %fusion.12 = (f32[1024]{0:T(1024)S(1)}, f32[1024]{0:T(1024)S(1)}) fusion(f32[1024,2048]{1,0:T(8,128)S(1)} %fusion.41, f32[1024]{0:T(1024)S(1)} %get-tuple-element.26, s32[2048]{0:T(1024)S(1)} %get-tuple-element.22, s32[1024]{0:T(1024)S(1)} %iota_add_fusion.1, s32[1024]{0:T(1024)S(1)} %copy-done.8, f32[1024]{0:T(1024)S(1)} %get-tuple-element.25, ...), kind=kLoop, calls=%fused_computation.21 | loop fusion | flops 33552384 | bytes 16826368 | tf_op jit(solution)/shard_map/reduce_sum | solution.py:69
  108.9 2.8 fusion.29
  111.7 8.0 %convolution_convert_fusion.1 = bf16[1024,2304]{1,0:T(8,128)(2,1)} fusion(bf16[64,2304]{1,0:T(8,128)(2,1)S(1)} %copy-done.11, f32[1024,64]{0,1:T(8,128)S(1)} %fusion.29, f32[1024,2048]{1,0:T(8,128)} %copy-done.4, f32[1024]{0:T(1024)S(1)} %get-tuple-element.25, s32[2048]{0:T(1024)S(1)} %iota_add_fusion, s32[2048]{0:T(1024)S(1)} %get-tuple-element.23, ...), kind=kOutput, calls=%fused_computation.17 | convolution fusion | flops 589758464 | bytes 13959168 | tf_op jit(solution)/shard_map/dot_general | solution.py:169
  119.8 55.1 %reduce-scatter.3.cloned.1.call-done = bf16[128,2304]{1,0:T(8,128)(2,1)} async-done(((bf16[1024,2304]{1,0:T(8,128)(2,1)}), bf16[128,2304]{1,0:T(8,128)(2,1)}) %reduce-scatter.3.cloned.1.call-update) | async-done | bytes 589840 | tf_op jit(solution)/shard_map/reduce_scatter | solution.py:168
  174.9 1.3 multiply_reduce_fusion
  176.3 1.3 multiply_convert_fusion.1
  177.6 11.1 %collective-permute-done = bf16[128,2304]{1,0:T(8,128)(2,1)S(1)} collective-permute-done((bf16[128,2304]{1,0:T(8,128)(2,1)S(1)}, bf16[128,2304]{1,0:T(8,128)(2,1)S(1)}, u32[]{:S(2)}, u32[]{:S(2)}) %collective-permute-start) | collective-permute-done | bytes 589856 | tf_op jit(solution)/shard_map/ppermute | solution.py:18
  188.7 3.5 collective-permute-start.4
  192.3 11.3 %collective-permute-done.1 = bf16[128,2304]{1,0:T(8,128)(2,1)S(1)} collective-permute-done((bf16[128,2304]{1,0:T(8,128)(2,1)S(1)}, bf16[128,2304]{1,0:T(8,128)(2,1)S(1)}, u32[]{:S(2)}, u32[]{:S(2)}) %collective-permute-start.1) | collective-permute-done | bytes 589856 | tf_op jit(solution)/shard_map/ppermute | solution.py:18
  203.6 12.8 %all_gather.15 = s32[1024,2]{0,1:T(2,128)S(1)} all-gather(s32[128,2]{0,1:T(2,128)S(1)} %copy-done.10), channel_id=1, replica_groups=mesh['seq'=4,'tensor'=8] {'tensor'}, dimensions={0}, use_global_device_ids=true | all-gather | bytes 9216 | tf_op jit(solution)/shard_map/all_gather | solution.py:182
  216.5 1.3 collective-permute-start.5
  218.4 12.9 %collective-permute-done.5 = bf16[128,2304]{1,0:T(8,128)(2,1)} collective-permute-done((bf16[128,2304]{1,0:T(8,128)(2,1)S(1)}, bf16[128,2304]{1,0:T(8,128)(2,1)}, u32[]{:S(2)}, u32[]{:S(2)}) %collective-permute-start.5) | collective-permute-done | bytes 589856 | tf_op jit(solution)/shard_map/ppermute | solution.py:20
  231.2 3.8 %collective-permute-start.6 = (bf16[128,2304]{1,0:T(8,128)(2,1)}, bf16[128,2304]{1,0:T(8,128)(2,1)S(1)}, u32[]{:S(2)}, u32[]{:S(2)}) collective-permute-start(bf16[128,2304]{1,0:T(8,128)(2,1)} %collective-permute-done.5), channel_id=1, source_target_pairs={{0,7},{1,0},{2,1},{3,2},{4,3},{5,4},{6,5},{7,6},{8,15},{9,8},{10,9... | collective-permute-start | bytes 1769480 | tf_op jit(solution)/shard_map/ppermute | solution.py:20
  236.1 1.1 constant_dynamic-update-slice_fusion.14
  238.6 4.2 %collective-permute-done.6 = bf16[128,2304]{1,0:T(8,128)(2,1)S(1)} collective-permute-done((bf16[128,2304]{1,0:T(8,128)(2,1)}, bf16[128,2304]{1,0:T(8,128)(2,1)S(1)}, u32[]{:S(2)}, u32[]{:S(2)}) %collective-permute-start.6) | collective-permute-done | bytes 589856 | tf_op jit(solution)/shard_map/ppermute | solution.py:20
  242.8 1.1 constant_dynamic-update-slice_fusion.7
  245.2 1.1 constant_dynamic-update-slice_fusion.1
  247.5 1.5 copy-done.3
  248.9 1.9 fusion.96
  251.1 12.5 %fusion.2 = f32[512,2880]{0,1:T(8,128)} fusion(bf16[512,2304]{1,0:T(8,128)(2,1)} %bitcast.66, bf16[2,2880,2304]{2,1,0:T(8,128)(2,1)} %param.16), kind=kOutput, calls=%fused_computation.2 | convolution fusion | flops 6794772480 | bytes 21528576 | tf_op jit(solution)/shard_map/dot_general | solution.py:102
  263.8 23.3 %fusion.11 = bf16[512,2304]{1,0:T(8,128)(2,1)} fusion(bf16[2880,2304]{1,0:T(8,128)(2,1)} %param.17, f32[512]{0:T(512)S(1)} %mul.197, f32[512,2880]{0,1:T(8,128)} %fusion.2, bf16[512,2304]{1,0:T(8,128)(2,1)} %bitcast.67, bf16[2,2880,2304]{2,1,0:T(8,128)(2,1)} %param.16), kind=kOutput, calls=%fused_computation.20 | convolution fusion | flops 13600751616 | bytes 37160960 | tf_op jit(solution)/shard_map/dot_general | solution.py:107
  287.1 5.3 %convolution_convert_fusion = bf16[8,128,2304]{2,1,0:T(8,128)(2,1)} fusion(bf16[8,64,2304]{2,1,0:T(8,128)(2,1)} %bitcast.68, s32[8,128]{1,0:T(8,128)S(1)} %broadcast_add_fusion, pred[8,128]{1,0:T(8,128)(4,1)S(1)} %broadcast_compare_fusion), kind=kOutput, calls=%fused_computation.16 | convolution fusion | flops 304480256 | bytes 7083008 | tf_op jit(solution)/shard_map/sjr,sjd->srd/dot_general | solution.py:205
  293.2 55.5 %reduce-scatter.5.cloned.1.call-done = bf16[128,2304]{1,0:T(8,128)(2,1)} async-done(((bf16[1024,2304]{1,0:T(8,128)(2,1)}), bf16[128,2304]{1,0:T(8,128)(2,1)}) %reduce-scatter.5.cloned.1.call-update) | async-done | bytes 589840 | tf_op jit(solution)/shard_map/reduce_scatter | solution.py:211
  348.7 2.1 add_convert_fusion
  (83 shorter events, 8.4 us)
Async XLA Ops:
  7.2 58.1 %copy-start = (bf16[3,2304,64]{1,2,0:T(8,128)(2,1)S(1)}, bf16[3,2304,64]{1,2,0:T(8,128)(2,1)}, u32[]{:S(2)}) copy-start(bf16[3,2304,64]{1,2,0:T(8,128)(2,1)} %param.13) | copy-start | bytes 2654212
  7.2 63.5 %copy-start.8 = (s32[1024]{0:T(1024)S(1)}, s32[1024]{0:T(1024)}, u32[]{:S(2)}) copy-start(s32[1024]{0:T(1024)} %param.18) | copy-start | bytes 12292
  7.2 58.1 %all-gather.3.cloned.1.call-start = ((), (), s32[]{:S(2)}) async-start(), calls=%async_computation.2 | async-start | bytes 5308416 | tf_op jit(solution)/shard_map/all_gather | solution.py:133
  10.7 85.6 %all-gather.5.cloned.1.call-start = ((), (), s32[]{:S(2)}) async-start(), calls=%async_computation.3 | async-start | bytes 1310720 | tf_op jit(solution)/shard_map/all_gather | solution.py:157
  70.7 104.2 %reduce-scatter.3.cloned.1.call-start = ((), (), s32[]{:S(2)}) async-start(), calls=%async_computation.4 | async-start | bytes 5308416 | tf_op jit(solution)/shard_map/reduce_scatter | solution.py:168
  96.3 2.3 copy-start.7
  102.7 6.2 %copy-start.4 = (f32[1024,2048]{1,0:T(8,128)}, f32[1024,2048]{1,0:T(8,128)S(1)}, u32[]{:S(2)}) copy-start(f32[1024,2048]{1,0:T(8,128)S(1)} %get-tuple-element.27) | copy-start | bytes 25165828
  108.9 2.8 copy-start.11
  111.7 63.2 %copy-start.2 = (bf16[128,2304]{1,0:T(8,128)(2,1)S(1)}, bf16[128,2304]{1,0:T(8,128)(2,1)}, u32[]{:S(2)}) copy-start(bf16[128,2304]{1,0:T(8,128)(2,1)} %param.10) | copy-start | bytes 1769476
  111.7 64.6 %copy-start.9 = (f32[2304]{0:T(1024)S(1)}, f32[2304]{0:T(1024)}, u32[]{:S(2)}) copy-start(f32[2304]{0:T(1024)} %param.12) | copy-start | bytes 27652
  111.7 91.9 %copy-start.10 = (s32[128,2]{0,1:T(2,128)S(1)}, s32[128,2]{0,1:T(2,128)}, u32[]{:S(2)}) copy-start(s32[128,2]{0,1:T(2,128)} %param.19) | copy-start | bytes 3076
  119.8 228.9 %reduce-scatter.5.cloned.1.call-start = ((), (), s32[]{:S(2)}) async-start(), calls=%async_computation.5 | async-start | bytes 5308416 | tf_op jit(solution)/shard_map/reduce_scatter | solution.py:211
  177.5 11.2 %collective-permute-start = (bf16[128,2304]{1,0:T(8,128)(2,1)S(1)}, bf16[128,2304]{1,0:T(8,128)(2,1)S(1)}, u32[]{:S(2)}, u32[]{:S(2)}) collective-permute-start(bf16[128,2304]{1,0:T(8,128)(2,1)S(1)} %multiply_convert_fusion.1), channel_id=1, source_target_pairs={{0,1},{1,2},{2,3},{3,4},{4,5},{5,6},{6,7},{7,0},{8,9},{9,10},{10,1... | collective-permute-start | bytes 1769480 | tf_op jit(solution)/shard_map/ppermute | solution.py:18
  188.7 14.9 %collective-permute-start.1 = (bf16[128,2304]{1,0:T(8,128)(2,1)S(1)}, bf16[128,2304]{1,0:T(8,128)(2,1)S(1)}, u32[]{:S(2)}, u32[]{:S(2)}) collective-permute-start(bf16[128,2304]{1,0:T(8,128)(2,1)S(1)} %collective-permute-done), channel_id=1, source_target_pairs={{0,1},{1,2},{2,3},{3,4},{4,5},{5,6},{6,7},{7,0},{8,9},{9,10},{10,1... | collective-permute-start | bytes 1769480 | tf_op jit(solution)/shard_map/ppermute | solution.py:18
  188.7 27.7 %collective-permute-start.4 = (bf16[128,2304]{1,0:T(8,128)(2,1)S(1)}, bf16[128,2304]{1,0:T(8,128)(2,1)S(1)}, u32[]{:S(2)}, u32[]{:S(2)}) collective-permute-start(bf16[128,2304]{1,0:T(8,128)(2,1)S(1)} %multiply_convert_fusion.1), channel_id=1, source_target_pairs={{0,7},{1,0},{2,1},{3,2},{4,3},{5,4},{6,5},{7,6},{8,15},{9,8},{10,9... | collective-permute-start | bytes 1769480 | tf_op jit(solution)/shard_map/ppermute | solution.py:20
  203.6 14.2 %collective-permute-start.2 = (bf16[128,2304]{1,0:T(8,128)(2,1)S(1)}, bf16[128,2304]{1,0:T(8,128)(2,1)}, u32[]{:S(2)}, u32[]{:S(2)}) collective-permute-start(bf16[128,2304]{1,0:T(8,128)(2,1)S(1)} %collective-permute-done.1), channel_id=1, source_target_pairs={{0,1},{1,2},{2,3},{3,4},{4,5},{5,6},{6,7},{7,0},{8,9},{9,10},{10,1... | collective-permute-start | bytes 1769480 | tf_op jit(solution)/shard_map/ppermute | solution.py:18
  216.5 14.8 %collective-permute-start.5 = (bf16[128,2304]{1,0:T(8,128)(2,1)S(1)}, bf16[128,2304]{1,0:T(8,128)(2,1)}, u32[]{:S(2)}, u32[]{:S(2)}) collective-permute-start(bf16[128,2304]{1,0:T(8,128)(2,1)S(1)} %collective-permute-done.4), channel_id=1, source_target_pairs={{0,7},{1,0},{2,1},{3,2},{4,3},{5,4},{6,5},{7,6},{8,15},{9,8},{10,9... | collective-permute-start | bytes 1769480 | tf_op jit(solution)/shard_map/ppermute | solution.py:20
  217.8 17.2 %collective-permute-start.3 = (bf16[128,2304]{1,0:T(8,128)(2,1)}, bf16[128,2304]{1,0:T(8,128)(2,1)}, u32[]{:S(2)}, u32[]{:S(2)}) collective-permute-start(bf16[128,2304]{1,0:T(8,128)(2,1)} %collective-permute-done.2), channel_id=1, source_target_pairs={{0,1},{1,2},{2,3},{3,4},{4,5},{5,6},{6,7},{7,0},{8,9},{9,10},{10,1... | collective-permute-start | bytes 1769480 | tf_op jit(solution)/shard_map/ppermute | solution.py:18
  231.2 11.5 %collective-permute-start.6 = (bf16[128,2304]{1,0:T(8,128)(2,1)}, bf16[128,2304]{1,0:T(8,128)(2,1)S(1)}, u32[]{:S(2)}, u32[]{:S(2)}) collective-permute-start(bf16[128,2304]{1,0:T(8,128)(2,1)} %collective-permute-done.5), channel_id=1, source_target_pairs={{0,7},{1,0},{2,1},{3,2},{4,3},{5,4},{6,5},{7,6},{8,15},{9,8},{10,9... | collective-permute-start | bytes 1769480 | tf_op jit(solution)/shard_map/ppermute | solution.py:20
  246.4 2.6 copy-start.6
  247.5 1.5 copy-start.3
  263.8 87.0 %copy-start.1 = (bf16[3,2304,64]{1,2,0:T(8,128)(2,1)S(1)}, bf16[3,2304,64]{1,2,0:T(8,128)(2,1)}, u32[]{:S(2)}) copy-start(bf16[3,2304,64]{1,2,0:T(8,128)(2,1)} %param.13) | copy-start | bytes 2654212
  287.1 61.6 %copy-start.5 = (bf16[128,2304]{1,0:T(8,128)(2,1)S(1)}, bf16[128,2304]{1,0:T(8,128)(2,1)}, u32[]{:S(2)}) copy-start(bf16[128,2304]{1,0:T(8,128)(2,1)} %reduce-scatter.3.cloned.1.call-done) | copy-start | bytes 1769476
Sparse Core Ops, SparseCore 0:
  10.8 54.3 all-gather.2
  70.8 25.4 all-gather.4
  119.9 54.9 reduce-scatter.2
  292.5 56.1 reduce-scatter.4
